TPU v7x, 32 devices: a whole 2x2x4 slice. The times are simulated.
32 devices in a mesh: lon: 4 (over z), lat: 4 (over x, core), rep: 2 (over y).
Axes of the slice: x: 2, y: 2, z: 4, core: 2. Of those that a mesh axis runs over, the one named last changes fastest.
Arguments:
- inputs: float32 [2, 64, 128, 256], P('rep', 'lat', 'lon'), may hold values from -6 to 6
- cotangent: float32 [2, 64, 128, 256], P('rep', 'lat', 'lon'), may hold values from -6 to 6
- first_weight: float32 [2304, 256], replicated, may hold values from -0.125 to 0.125
- second_weight: float32 [2304, 256], replicated, may hold values from -0.125 to 0.125
Outputs:
- output: float32 [2, 64, 128, 256], P('rep', 'lat', 'lon')
- input_grad: float32 [2, 64, 128, 256], P('rep', 'lat', 'lon')
- first_grad: float32 [2304, 256], P('lon', ('lat', 'rep'))
- second_grad: float32 [2304, 256], P('lon', ('lat', 'rep'))
All inputs are finite; a program needn't handle non-finite values.
Results may differ from a plain program's by a relative error of at most 0.00012.
Values sent between devices are 32-bit elements; how exact they have to be, the bound alone decides.
No kernel may reach another device: no remote copies, remote signals or barrier semaphores. Data moves between devices by JAX's collectives and lax.ppermute only.
A program may use at most 128 MiB of HBM per device.

v0:
```python
import math

import jax
import jax.numpy as jnp
from jax import lax
from jax.sharding import PartitionSpec as P

HIGH = lax.Precision.HIGH


def shift_perm(count, periodic):
    forward = [(i, i + 1) for i in range(count - 1)]
    if periodic:
        forward.append((count - 1, 0))
    return forward, [(b, a) for a, b in forward]


def halo(block, axis, dim, width, periodic):
    forward, backward = shift_perm(lax.axis_size(axis), periodic)
    size = block.shape[dim]
    low = lax.ppermute(lax.slice_in_dim(block, size - width, size, axis=dim), axis, forward)
    high = lax.ppermute(lax.slice_in_dim(block, 0, width, axis=dim), axis, backward)
    return jnp.concatenate([low, block, high], axis=dim)


def taps_of(padded, rows, cols, flipped):
    pieces = []
    for a in range(3):
        for b in range(3):
            r, c = (2 - a, 2 - b) if flipped else (a, b)
            pieces.append(padded[r : r + rows, c : c + cols, :])
    return jnp.concatenate(pieces, axis=-1).reshape(rows * cols, -1)


def matmul(taps, weights):
    return jnp.dot(taps, weights, precision=HIGH, preferred_element_type=jnp.float32)


def transpose_kernel(weights):
    channels = weights.shape[1]
    stacked = weights.reshape(9, channels, channels)
    return jnp.swapaxes(stacked, 1, 2).reshape(9 * channels, channels)


def silu_slope(value):
    sigma = jax.nn.sigmoid(value)
    return sigma * (1.0 + value * (1.0 - sigma))


def kernel_grad_t(taps, grad_out):
    return jnp.einsum(
        "rd,rk->dk", grad_out, taps, precision=HIGH, preferred_element_type=jnp.float32
    )


def xor_perm(count, bit):
    return [(i, i ^ bit) for i in range(count)]


def pick(array, index, axis):
    return lax.dynamic_index_in_dim(array, index, axis, keepdims=False)


def scatter_sum(part):
    channels, taps = part.shape
    lon, lat, rep = lax.axis_size("lon"), lax.axis_size("lat"), lax.axis_size("rep")
    here_lat, here_rep, here_lon = (lax.axis_index(a) for a in ("lat", "rep", "lon"))
    x, core, y = here_lat // 2, here_lat % 2, here_rep
    each = channels // (lat * rep)
    view = part.reshape(2, 2, 2, each, taps)
    half = lax.ppermute(pick(view, 1 - core, 1), "lat", xor_perm(lat, 1))
    held = (pick(view, core, 1) + half).reshape(2, 2, 2, each // 2, taps)
    ahead, behind = held[:, :, 0], held[:, :, 1]
    got_0 = lax.ppermute(pick(ahead, 1 - y, 1), "rep", xor_perm(rep, 1))
    got_1 = lax.ppermute(pick(behind, 1 - x, 0), "lat", xor_perm(lat, 2))
    sum_0 = pick(ahead, y, 1) + got_0
    sum_1 = pick(behind, x, 0) + got_1
    got_0 = lax.ppermute(pick(sum_0, 1 - x, 0), "lat", xor_perm(lat, 2))
    got_1 = lax.ppermute(pick(sum_1, 1 - y, 0), "rep", xor_perm(rep, 1))
    tail = jnp.concatenate([pick(sum_0, x, 0) + got_0, pick(sum_1, y, 0) + got_1], axis=0)
    if lon & (lon - 1) or lon > 8:
        return lax.psum_scatter(tail, "lon", scatter_dimension=1, tiled=True).T
    blocks = jnp.swapaxes(tail.reshape(each, lon, taps // lon), 0, 1)
    total = pick(blocks, here_lon, 0)
    for step in range(1, lon):
        total = total + lax.ppermute(
            pick(blocks, here_lon ^ step, 0), "lon", xor_perm(lon, step)
        )
    return total.T


def local(inputs, cotangent, first_weight, second_weight):
    channels = inputs.shape[3]
    rows, cols = inputs.shape[1], inputs.shape[2]
    here = inputs[0]
    grad = cotangent[0]
    first_back = transpose_kernel(first_weight)
    second_back = transpose_kernel(second_weight)
    both = jnp.concatenate([here, grad], axis=-1)
    both = halo(both, "lat", 0, 2, False)
    both = halo(both, "lon", 1, 2, True)
    wide_in, wide_cot = both[..., :channels], both[..., channels:]
    row = lax.axis_index("lat") * rows - 1 + jnp.arange(rows + 2)
    inside = ((row >= 0) & (row < rows * lax.axis_size("lat")))[:, None, None]
    er, ec = rows + 2, cols + 2
    act_in = jax.nn.silu(wide_in)
    hidden = matmul(taps_of(act_in, er, ec, False), first_weight).reshape(er, ec, channels)
    act_hidden = jnp.where(inside, jax.nn.silu(hidden), 0.0)
    second_taps = taps_of(act_hidden, rows, cols, False)
    scale = 1.0 / math.sqrt(
        rows * cols * lax.axis_size("rep") * lax.axis_size("lat") * lax.axis_size("lon")
    )
    second_part = kernel_grad_t(second_taps, grad.reshape(rows * cols, channels)) * scale
    second_grad = scatter_sum(second_part)
    hidden_grad = matmul(taps_of(wide_cot, er, ec, True), second_back).reshape(er, ec, channels)
    hidden_grad = jnp.where(inside, hidden_grad * silu_slope(hidden), 0.0)
    first_taps = taps_of(act_in[1:-1, 1:-1], rows, cols, False)
    first_part = (
        kernel_grad_t(first_taps, hidden_grad[1:-1, 1:-1].reshape(rows * cols, channels)) * scale
    )
    first_grad = scatter_sum(first_part)
    output = inputs + matmul(second_taps, second_weight).reshape(inputs.shape)
    back = matmul(taps_of(hidden_grad, rows, cols, True), first_back).reshape(inputs.shape)
    input_grad = cotangent + back * silu_slope(inputs)
    return (output, input_grad, first_grad, second_grad)


def solution(mesh):
    in_specs = (P("rep", "lat", "lon", None), P("rep", "lat", "lon", None), P(), P())
    out_specs = (
        P("rep", "lat", "lon", None),
        P("rep", "lat", "lon", None),
        P("lon", ("lat", "rep")),
        P("lon", ("lat", "rep")),
    )
    return jax.shard_map(local, mesh=mesh, in_specs=in_specs, out_specs=out_specs, check_vma=False)
```

profile of v0, /device:TPU:0, one launch (start us, length us, event | category | flops | bytes accessed | tf_op | source)
XLA Modules:
  0.0 93.5 jit_solution(4495470042969253115)
XLA Ops:
  0.6 1.8 %pad_maximum_fusion.5 = (f32[2,32,512]{2,1,0:T(8,128)}, f32[2,32,512]{2,1,0:T(8,128)}) fusion(f32[16,32,256]{2,1,0:T(8,128)} %bitcast.140, f32[16,32,256]{2,1,0:T(8,128)} %bitcast.136), kind=kLoop, calls=%fused_computation.89 | loop fusion | flops 65536 | bytes 1310720 | tf_op jit(solution)/shard_map/slice | solution.py:21
  2.4 2.4 %collective-permute-start = (f32[2,32,512]{2,1,0:T(8,128)}, f32[2,32,512]{2,1,0:T(8,128)S(1)}, u32[]{:S(2)}, u32[]{:S(2)}) collective-permute-start(f32[2,32,512]{2,1,0:T(8,128)} %get-tuple-element.12), channel_id=1, source_target_pairs={{0,2},{2,4},{4,6},{1,3},{3,5},{5,7},{8,10},{10,12},{12,14},{9,11},... | collective-permute-start | bytes 393224 | tf_op jit(solution)/shard_map/ppermute | solution.py:21
  4.8 1.3 %collective-permute-start.1 = (f32[2,32,512]{2,1,0:T(8,128)}, f32[2,32,512]{2,1,0:T(8,128)}, u32[]{:S(2)}, u32[]{:S(2)}) collective-permute-start(f32[2,32,512]{2,1,0:T(8,128)} %get-tuple-element.13), channel_id=1, source_target_pairs={{2,0},{4,2},{6,4},{3,1},{5,3},{7,5},{10,8},{12,10},{14,12},{11,9},... | collective-permute-start | bytes 393224 | tf_op jit(solution)/shard_map/ppermute | solution.py:22
  6.2 3.1 %copy.12 = f32[9,256,256]{2,1,0:T(8,128)} copy(f32[9,256,256]{1,2,0:T(8,128)} %bitcast.146) | data formatting | bytes 4718592 | tf_op jit(solution)/shard_map/transpose | solution.py:42
  9.3 2.0 %copy.13 = f32[9,256,256]{2,1,0:T(8,128)} copy(f32[9,256,256]{1,2,0:T(8,128)S(1)} %bitcast.145) | data formatting | bytes 4718592 | tf_op jit(solution)/shard_map/transpose | solution.py:42
  11.3 0.8 pad_maximum_fusion.9
  12.2 2.5 %collective-permute-start.2 = (f32[20,2,512]{2,1,0:T(2,128)S(1)}, f32[20,2,512]{2,1,0:T(2,128)S(1)}, u32[]{:S(2)}, u32[]{:S(2)}) collective-permute-start(f32[20,2,512]{2,1,0:T(2,128)S(1)} %get-tuple-element.6), channel_id=1, source_target_pairs={{0,8},{8,16},{16,24},{24,0},{1,9},{9,17},{17,25},{25,1},{2,10},{10... | collective-permute-start | bytes 245768 | tf_op jit(solution)/shard_map/ppermute | solution.py:21
  14.6 2.1 %collective-permute-start.3 = (f32[20,2,512]{2,1,0:T(2,128)S(1)}, f32[20,2,512]{2,1,0:T(2,128)S(1)}, u32[]{:S(2)}, u32[]{:S(2)}) collective-permute-start(f32[20,2,512]{2,1,0:T(2,128)S(1)} %get-tuple-element.7), channel_id=1, source_target_pairs={{8,0},{16,8},{24,16},{0,24},{9,1},{17,9},{25,17},{1,25},{10,2},{18... | collective-permute-start | bytes 245768 | tf_op jit(solution)/shard_map/ppermute | solution.py:22
  16.7 2.5 %collective-permute-done.2 = f32[20,2,512]{2,1,0:T(2,128)S(1)} collective-permute-done((f32[20,2,512]{2,1,0:T(2,128)S(1)}, f32[20,2,512]{2,1,0:T(2,128)S(1)}, u32[]{:S(2)}, u32[]{:S(2)}) %collective-permute-start.2) | collective-permute-done | bytes 81952 | tf_op jit(solution)/shard_map/ppermute | solution.py:21
  19.2 2.2 %collective-permute-done.3 = f32[20,2,512]{2,1,0:T(2,128)S(1)} collective-permute-done((f32[20,2,512]{2,1,0:T(2,128)S(1)}, f32[20,2,512]{2,1,0:T(2,128)S(1)}, u32[]{:S(2)}, u32[]{:S(2)}) %collective-permute-start.3) | collective-permute-done | bytes 81952 | tf_op jit(solution)/shard_map/ppermute | solution.py:22
  21.4 1.2 %pad_maximum_fusion = f32[20,36,512]{2,1,0:T(8,128)S(1)} fusion(f32[20,2,512]{2,1,0:T(2,128)S(1)} %collective-permute-done.3, f32[2,32,512]{2,1,0:T(8,128)} %collective-permute-done.1, f32[16,32,256]{2,1,0:T(8,128)S(1)} %bitcast.142, f32[16,32,256]{2,1,0:T(8,128)S(1)} %bitcast.138, f32[2,32,512]{2,1,0:T(8,128)S(1)} %collective-permute-done, ...), kind=kLoop, calls=%fused_computation.7 | loop fusion | flops 1843200 | bytes 2949120 | tf_op jit(solution)/shard_map/concatenate | solution.py:23
  22.6 0.2 divide_multiply_fusion
  23.0 1.4 %maximum_maximum_fusion = (f32[20,34,512]{2,1,0:T(8,128)S(1)}, f32[20,34,512]{2,1,0:T(8,128)S(1)}) fusion(f32[2,32,512]{2,1,0:T(8,128)} %collective-permute-done.1, f32[16,32,256]{2,1,0:T(8,128)S(1)} %bitcast.143, f32[16,32,256]{2,1,0:T(8,128)S(1)} %bitcast.139, f32[2,32,512]{2,1,0:T(8,128)S(1)} %collective-permute-done, ...), kind=kLoop, calls=%fused_computation.9 | loop fusion | flops 2785280 | bytes 4259840 | tf_op jit(solution)/shard_map/concatenate | solution.py:23
  24.4 0.1 slice_dynamic-update-slice_fusion.7
  24.5 0.1 slice_dynamic-update-slice_fusion.6
  24.7 0.1 slice_dynamic-update-slice_fusion.4
  24.8 0.1 slice_dynamic-update-slice_fusion.3
  24.9 0.1 slice_dynamic-update-slice_fusion.1
  25.0 0.1 slice_dynamic-update-slice_fusion
  26.1 2.9 %multiply_select_fusion = (f32[18,34,256]{2,1,0:T(8,128)S(1)}, f32[18,34,256]{2,1,0:T(8,128)S(1)}) fusion(pred[18]{0:T(512)(128)(4,1)S(1)} %compare_and_fusion, f32[18,34,2304]{2,1,0:T(8,128)S(1)} %slice_dynamic-update-slice_fusion.9, f32[2304,256]{1,0:T(8,128)S(1)} %copy-done.3), kind=kOutput, calls=%fused_computation.40 | convolution fusion | flops 2166617088 | bytes 9252882 | tf_op jit(solution)/shard_map/dot_general | solution.py:36
  29.0 2.9 %fusion.5 = f32[18,34,256]{2,1,0:T(8,128)S(1)} fusion(f32[18,34,2304]{2,1,0:T(8,128)S(1)} %slice_dynamic-update-slice_fusion, f32[2304,256,1]{1,0,2:T(8,128)S(1)} %bitcast.148, f32[18,34,256]{2,1,0:T(8,128)S(1)} %get-tuple-element.23, pred[18]{0:T(512)(128)(4,1)S(1)} %compare_and_fusion), kind=kOutput, calls=%fused_computation.11 | convolution fusion | flops 2167243776 | bytes 9252882 | tf_op jit(solution)/shard_map/dot_general | solution.py:36
  32.0 2.7 %fusion = f32[256,2304]{1,0:T(8,128)S(1)} fusion(f32[16,32,2304]{2,1,0:T(8,128)S(1)} %slice_dynamic-update-slice_fusion.18, f32[18,34,256]{2,1,0:T(8,128)S(1)} %fusion.5), kind=kOutput, calls=%fused_computation.2 | convolution fusion | flops 1812529152 | bytes 7602176 | tf_op jit(solution)/shard_map/rd,rk->dk/dot_general | solution.py:51
  34.7 0.1 dynamic-slice_bitcast_fusion.1
  34.8 0.2 collective-permute-start.4
  35.6 2.5 %convolution_multiply_fusion = f32[2304,256]{0,1:T(8,128)S(1)} fusion(f32[512,2304]{1,0:T(8,128)S(1)} %bitcast.135, f32[512,256]{1,0:T(8,128)S(1)} %bitcast.144), kind=kOutput, calls=%fused_computation | convolution fusion | flops 1812529152 | bytes 7602176 | tf_op jit(solution)/shard_map/rd,rk->dk/dot_general | solution.py:51
  38.1 0.1 dynamic-slice_bitcast_fusion
  38.2 0.5 collective-permute-start.12
  39.2 0.7 copy-done.5
  39.9 2.9 %fusion.10 = f32[1,16,32,256]{3,2,1,0:T(8,128)} fusion(f32[1,16,32,256]{3,2,1,0:T(8,128)S(1)} %copy-done.2, f32[16,32,2304]{2,1,0:T(8,128)S(1)} %slice_dynamic-update-slice_fusion.27, f32[2304,256,1]{1,0,2:T(8,128)S(1)} %bitcast.147, f32[1,16,32,256]{3,2,1,0:T(8,128)S(1)} %copy-done.1), kind=kOutput, calls=%fused_computation.15 | convolution fusion | flops 1813118976 | bytes 8650752 | tf_op jit(solution)/shard_map/dot_general | solution.py:36
  42.8 0.1 bitcast_add_fusion.1
  43.0 0.1 fusion.22
  43.1 1.6 %collective-permute-start.5 = (f32[2,16,2304]{2,1,0:T(8,128)S(1)}, f32[2,16,2304]{2,1,0:T(8,128)S(1)}, u32[]{:S(2)}, u32[]{:S(2)}) collective-permute-start(f32[2,16,2304]{2,1,0:T(8,128)S(1)} %dynamic-slice_bitcast_fusion.5), channel_id=1, source_target_pairs={{0,1},{1,0},{2,3},{3,2},{4,5},{5,4},{6,7},{7,6},{8,9},{9,8},{10,11... | collective-permute-start | bytes 884744 | tf_op jit(solution)/shard_map/ppermute | solution.py:74
  44.7 2.8 %collective-permute-start.7 = (f32[2,16,2304]{2,1,0:T(8,128)S(1)}, f32[2,16,2304]{2,1,0:T(8,128)S(1)}, u32[]{:S(2)}, u32[]{:S(2)}) collective-permute-start(f32[2,16,2304]{2,1,0:T(8,128)S(1)} %dynamic-slice_bitcast_fusion.4), channel_id=1, source_target_pairs={{0,4},{2,6},{4,0},{6,2},{1,5},{3,7},{5,1},{7,3},{8,12},{10,14},{12... | collective-permute-start | bytes 884744 | tf_op jit(solution)/shard_map/ppermute | solution.py:75
  47.4 0.1 bitcast_add_fusion
  47.6 0.1 fusion.21
  47.7 0.6 collective-permute-start.13
  48.3 0.1 collective-permute-start.15
  48.4 4.6 %collective-permute-done.5 = f32[2,16,2304]{2,1,0:T(8,128)S(1)} collective-permute-done((f32[2,16,2304]{2,1,0:T(8,128)S(1)}, f32[2,16,2304]{2,1,0:T(8,128)S(1)}, u32[]{:S(2)}, u32[]{:S(2)}) %collective-permute-start.5) | collective-permute-done | bytes 294944 | tf_op jit(solution)/shard_map/ppermute | solution.py:74
  53.1 2.7 %collective-permute-start.6 = (f32[16,2304]{1,0:T(8,128)S(1)}, f32[16,2304]{1,0:T(8,128)S(1)}, u32[]{:S(2)}, u32[]{:S(2)}) collective-permute-start(f32[16,2304]{1,0:T(8,128)S(1)} %dynamic-slice_bitcast_fusion.9), channel_id=1, source_target_pairs={{0,4},{2,6},{4,0},{6,2},{1,5},{3,7},{5,1},{7,3},{8,12},{10,14},{12... | collective-permute-start | bytes 442376 | tf_op jit(solution)/shard_map/ppermute | solution.py:78
  55.8 1.6 %collective-permute-start.8 = (f32[16,2304]{1,0:T(8,128)S(1)}, f32[16,2304]{1,0:T(8,128)S(1)}, u32[]{:S(2)}, u32[]{:S(2)}) collective-permute-start(f32[16,2304]{1,0:T(8,128)S(1)} %dynamic-slice_bitcast_fusion.8), channel_id=1, source_target_pairs={{0,1},{1,0},{2,3},{3,2},{4,5},{5,4},{6,7},{7,6},{8,9},{9,8},{10,11... | collective-permute-start | bytes 442376 | tf_op jit(solution)/shard_map/ppermute | solution.py:79
  57.4 1.9 %collective-permute-done.13 = f32[2,16,2304]{2,1,0:T(8,128)S(1)} collective-permute-done((f32[2,16,2304]{2,1,0:T(8,128)S(1)}, f32[2,16,2304]{2,1,0:T(8,128)S(1)}, u32[]{:S(2)}, u32[]{:S(2)}) %collective-permute-start.13) | collective-permute-done | bytes 294944 | tf_op jit(solution)/shard_map/ppermute | solution.py:74
  59.4 2.7 %collective-permute-start.14 = (f32[16,2304]{1,0:T(8,128)S(1)}, f32[16,2304]{1,0:T(8,128)S(1)}, u32[]{:S(2)}, u32[]{:S(2)}) collective-permute-start(f32[16,2304]{1,0:T(8,128)S(1)} %dynamic-slice_bitcast_fusion.7), channel_id=1, source_target_pairs={{0,4},{2,6},{4,0},{6,2},{1,5},{3,7},{5,1},{7,3},{8,12},{10,14},{12... | collective-permute-start | bytes 442376 | tf_op jit(solution)/shard_map/ppermute | solution.py:78
  62.1 0.7 dynamic-slice_bitcast_fusion.6
  62.8 1.5 %collective-permute-start.16 = (f32[16,2304]{1,0:T(8,128)}, f32[16,2304]{1,0:T(8,128)}, u32[]{:S(2)}, u32[]{:S(2)}) collective-permute-start(f32[16,2304]{1,0:T(8,128)} %dynamic-slice_bitcast_fusion.6), channel_id=1, source_target_pairs={{0,1},{1,0},{2,3},{3,2},{4,5},{5,4},{6,7},{7,6},{8,9},{9,8},{10,11... | collective-permute-start | bytes 442376 | tf_op jit(solution)/shard_map/ppermute | solution.py:79
  64.3 0.4 collective-permute-done.6
  64.7 2.7 %collective-permute-done.14 = f32[16,2304]{1,0:T(8,128)S(1)} collective-permute-done((f32[16,2304]{1,0:T(8,128)S(1)}, f32[16,2304]{1,0:T(8,128)S(1)}, u32[]{:S(2)}, u32[]{:S(2)}) %collective-permute-start.14) | collective-permute-done | bytes 147488 | tf_op jit(solution)/shard_map/ppermute | solution.py:78
  67.5 0.7 bitcast_add_fusion.7
  68.1 0.7 pad_maximum_fusion.2
  68.9 1.2 %reshape.109 = f32[32,4,576]{2,1,0:T(4,128)S(1)} reshape(f32[32,2304]{1,0:T(8,128)} %pad_maximum_fusion.2) | data formatting | bytes 589824 | tf_op jit(solution)/shard_map/reshape | solution.py:83
  70.1 0.9 bitcast_add_fusion.6
  71.0 1.6 %pad_maximum_fusion.3 = f32[32,2304]{1,0:T(8,128)} fusion(f32[16,2304]{1,0:T(8,128)S(1)} %bitcast_add_fusion.6, f32[16,2304]{1,0:T(8,128)} %bitcast_add_fusion.7), kind=kLoop, calls=%fused_computation.71 | loop fusion | flops 73728 | bytes 589824 | tf_op jit(solution)/shard_map/concatenate | solution.py:80
  72.7 1.2 %reshape.113 = f32[32,4,576]{2,1,0:T(4,128)S(1)} reshape(f32[32,2304]{1,0:T(8,128)} %pad_maximum_fusion.3) | data formatting | bytes 589824 | tf_op jit(solution)/shard_map/reshape | solution.py:83
  73.9 0.6 constant_dynamic-slice_fusion.3
  74.5 1.0 %collective-permute-start.17 = (f32[32,576]{1,0:T(8,128)S(1)}, f32[32,576]{1,0:T(8,128)S(1)}, u32[]{:S(2)}, u32[]{:S(2)}) collective-permute-start(f32[32,576]{1,0:T(8,128)S(1)} %bitcast.157), channel_id=1, source_target_pairs={{0,8},{8,0},{16,24},{24,16},{1,9},{9,1},{17,25},{25,17},{2,10},{10... | collective-permute-start | bytes 221192 | tf_op jit(solution)/shard_map/ppermute | solution.py:86
  75.5 2.5 %collective-permute-start.18 = (f32[32,576]{1,0:T(8,128)S(1)}, f32[32,576]{1,0:T(8,128)S(1)}, u32[]{:S(2)}, u32[]{:S(2)}) collective-permute-start(f32[32,576]{1,0:T(8,128)S(1)} %bitcast.155), channel_id=1, source_target_pairs={{0,16},{8,24},{16,0},{24,8},{1,17},{9,25},{17,1},{25,9},{2,18},{10... | collective-permute-start | bytes 221192 | tf_op jit(solution)/shard_map/ppermute | solution.py:86
  78.0 0.9 collective-permute-start.19
  79.0 5.2 %fusion.11 = f32[1,16,32,256]{3,2,1,0:T(8,128)} fusion(f32[1,16,32,256]{3,2,1,0:T(8,128)S(1)} %copy-done.1, f32[16,32,2304]{2,1,0:T(8,128)} %copy-done, f32[2304,256]{1,0:T(8,128)S(1)} %copy-done.4), kind=kOutput, calls=%fused_computation.16 | convolution fusion | flops 1812070400 | bytes 8126464 | tf_op jit(solution)/shard_map/dot_general | solution.py:36
  84.1 0.6 collective-permute-start.10
  84.8 2.4 %collective-permute-start.11 = (f32[32,576]{1,0:T(8,128)S(1)}, f32[32,576]{1,0:T(8,128)S(1)}, u32[]{:S(2)}, u32[]{:S(2)}) collective-permute-start(f32[32,576]{1,0:T(8,128)S(1)} %bitcast.159), channel_id=1, source_target_pairs={{0,24},{8,16},{16,8},{24,0},{1,25},{9,17},{17,9},{25,1},{2,26},{10... | collective-permute-start | bytes 221192 | tf_op jit(solution)/shard_map/ppermute | solution.py:86
  87.1 0.6 collective-permute-start.9
  87.7 0.7 fusion.17
  88.4 4.2 %collective-permute-done.10 = f32[32,576]{1,0:T(8,128)S(1)} collective-permute-done((f32[32,576]{1,0:T(8,128)S(1)}, f32[32,576]{1,0:T(8,128)S(1)}, u32[]{:S(2)}, u32[]{:S(2)}) %collective-permute-start.10) | collective-permute-done | bytes 73760 | tf_op jit(solution)/shard_map/ppermute | solution.py:86
  92.6 0.3 collective-permute-done.9
  92.8 0.7 fusion.20
  (84 shorter events, 2.6 us)
Async XLA Ops:
  0.6 8.7 %copy-start.3 = (f32[2304,256]{1,0:T(8,128)S(1)}, f32[2304,256]{1,0:T(8,128)}, u32[]{:S(2)}) copy-start(f32[2304,256]{1,0:T(8,128)} %param.6) | copy-start | bytes 7077892
  2.4 8.9 %collective-permute-start = (f32[2,32,512]{2,1,0:T(8,128)}, f32[2,32,512]{2,1,0:T(8,128)S(1)}, u32[]{:S(2)}, u32[]{:S(2)}) collective-permute-start(f32[2,32,512]{2,1,0:T(8,128)} %get-tuple-element.12), channel_id=1, source_target_pairs={{0,2},{2,4},{4,6},{1,3},{3,5},{5,7},{8,10},{10,12},{12,14},{9,11},... | collective-permute-start | bytes 393224 | tf_op jit(solution)/shard_map/ppermute | solution.py:21
  4.8 6.5 %collective-permute-start.1 = (f32[2,32,512]{2,1,0:T(8,128)}, f32[2,32,512]{2,1,0:T(8,128)}, u32[]{:S(2)}, u32[]{:S(2)}) collective-permute-start(f32[2,32,512]{2,1,0:T(8,128)} %get-tuple-element.13), channel_id=1, source_target_pairs={{2,0},{4,2},{6,4},{3,1},{5,3},{7,5},{10,8},{12,10},{14,12},{11,9},... | collective-permute-start | bytes 393224 | tf_op jit(solution)/shard_map/ppermute | solution.py:22
  6.2 5.2 %copy-start.1 = (f32[1,16,32,256]{3,2,1,0:T(8,128)S(1)}, f32[1,16,32,256]{3,2,1,0:T(8,128)}, u32[]{:S(2)}) copy-start(f32[1,16,32,256]{3,2,1,0:T(8,128)} %param.4) | copy-start | bytes 1572868
  6.2 5.2 %copy-start.2 = (f32[1,16,32,256]{3,2,1,0:T(8,128)S(1)}, f32[1,16,32,256]{3,2,1,0:T(8,128)}, u32[]{:S(2)}) copy-start(f32[1,16,32,256]{3,2,1,0:T(8,128)} %param.5) | copy-start | bytes 1572868
  12.2 7.0 %collective-permute-start.2 = (f32[20,2,512]{2,1,0:T(2,128)S(1)}, f32[20,2,512]{2,1,0:T(2,128)S(1)}, u32[]{:S(2)}, u32[]{:S(2)}) collective-permute-start(f32[20,2,512]{2,1,0:T(2,128)S(1)} %get-tuple-element.6), channel_id=1, source_target_pairs={{0,8},{8,16},{16,24},{24,0},{1,9},{9,17},{17,25},{25,1},{2,10},{10... | collective-permute-start | bytes 245768 | tf_op jit(solution)/shard_map/ppermute | solution.py:21
  14.6 6.8 %collective-permute-start.3 = (f32[20,2,512]{2,1,0:T(2,128)S(1)}, f32[20,2,512]{2,1,0:T(2,128)S(1)}, u32[]{:S(2)}, u32[]{:S(2)}) collective-permute-start(f32[20,2,512]{2,1,0:T(2,128)S(1)} %get-tuple-element.7), channel_id=1, source_target_pairs={{8,0},{16,8},{24,16},{0,24},{9,1},{17,9},{25,17},{1,25},{10,2},{18... | collective-permute-start | bytes 245768 | tf_op jit(solution)/shard_map/ppermute | solution.py:22
  26.1 2.9 %copy-start.6 = (f32[9,256,256]{2,1,0:T(8,128)S(1)}, f32[9,256,256]{2,1,0:T(8,128)}, u32[]{:S(2)}) copy-start(f32[9,256,256]{2,1,0:T(8,128)} %copy.12) | copy-start | bytes 7077892
  34.8 8.0 %collective-permute-start.4 = (f32[2,2,32,2304]{3,2,1,0:T(8,128)S(1)}, f32[2,2,32,2304]{3,2,1,0:T(8,128)S(1)}, u32[]{:S(2)}, u32[]{:S(2)}) collective-permute-start(f32[2,2,32,2304]{3,2,1,0:T(8,128)S(1)} %dynamic-slice_bitcast_fusion.1), channel_id=1, source_target_pairs={{0,2},{2,0},{4,6},{6,4},{1,3},{3,1},{5,7},{7,5},{8,10},{10,8},{12,... | collective-permute-start | bytes 3538952 | tf_op jit(solution)/shard_map/ppermute | solution.py:71
  35.5 2.7 %copy-start = (f32[16,32,2304]{2,1,0:T(8,128)}, f32[16,32,2304]{2,1,0:T(8,128)S(1)}, u32[]{:S(2)}) copy-start(f32[16,32,2304]{2,1,0:T(8,128)S(1)} %slice_dynamic-update-slice_fusion.35) | copy-start | bytes 14155780
  38.2 1.7 %copy-start.5 = (f32[9,256,256]{2,1,0:T(8,128)S(1)}, f32[9,256,256]{2,1,0:T(8,128)}, u32[]{:S(2)}) copy-start(f32[9,256,256]{2,1,0:T(8,128)} %copy.13) | copy-start | bytes 7077892
  38.2 9.2 %collective-permute-start.12 = (f32[2,2,32,2304]{3,2,1,0:T(8,128)S(1)}, f32[2,2,32,2304]{3,2,1,0:T(8,128)S(1)}, u32[]{:S(2)}, u32[]{:S(2)}) collective-permute-start(f32[2,2,32,2304]{3,2,1,0:T(8,128)S(1)} %dynamic-slice_bitcast_fusion), channel_id=1, source_target_pairs={{0,2},{2,0},{4,6},{6,4},{1,3},{3,1},{5,7},{7,5},{8,10},{10,8},{12,... | collective-permute-start | bytes 3538952 | tf_op jit(solution)/shard_map/ppermute | solution.py:71
  43.1 9.9 %collective-permute-start.5 = (f32[2,16,2304]{2,1,0:T(8,128)S(1)}, f32[2,16,2304]{2,1,0:T(8,128)S(1)}, u32[]{:S(2)}, u32[]{:S(2)}) collective-permute-start(f32[2,16,2304]{2,1,0:T(8,128)S(1)} %dynamic-slice_bitcast_fusion.5), channel_id=1, source_target_pairs={{0,1},{1,0},{2,3},{3,2},{4,5},{5,4},{6,7},{7,6},{8,9},{9,8},{10,11... | collective-permute-start | bytes 884744 | tf_op jit(solution)/shard_map/ppermute | solution.py:74
  44.7 11.1 %collective-permute-start.7 = (f32[2,16,2304]{2,1,0:T(8,128)S(1)}, f32[2,16,2304]{2,1,0:T(8,128)S(1)}, u32[]{:S(2)}, u32[]{:S(2)}) collective-permute-start(f32[2,16,2304]{2,1,0:T(8,128)S(1)} %dynamic-slice_bitcast_fusion.4), channel_id=1, source_target_pairs={{0,4},{2,6},{4,0},{6,2},{1,5},{3,7},{5,1},{7,3},{8,12},{10,14},{12... | collective-permute-start | bytes 884744 | tf_op jit(solution)/shard_map/ppermute | solution.py:75
  47.7 11.6 %collective-permute-start.13 = (f32[2,16,2304]{2,1,0:T(8,128)S(1)}, f32[2,16,2304]{2,1,0:T(8,128)S(1)}, u32[]{:S(2)}, u32[]{:S(2)}) collective-permute-start(f32[2,16,2304]{2,1,0:T(8,128)S(1)} %dynamic-slice_bitcast_fusion.3), channel_id=1, source_target_pairs={{0,1},{1,0},{2,3},{3,2},{4,5},{5,4},{6,7},{7,6},{8,9},{9,8},{10,11... | collective-permute-start | bytes 884744 | tf_op jit(solution)/shard_map/ppermute | solution.py:74
  48.3 13.8 %collective-permute-start.15 = (f32[2,16,2304]{2,1,0:T(8,128)S(1)}, f32[2,16,2304]{2,1,0:T(8,128)S(1)}, u32[]{:S(2)}, u32[]{:S(2)}) collective-permute-start(f32[2,16,2304]{2,1,0:T(8,128)S(1)} %dynamic-slice_bitcast_fusion.2), channel_id=1, source_target_pairs={{0,4},{2,6},{4,0},{6,2},{1,5},{3,7},{5,1},{7,3},{8,12},{10,14},{12... | collective-permute-start | bytes 884744 | tf_op jit(solution)/shard_map/ppermute | solution.py:75
  53.1 25.9 %copy-start.4 = (f32[2304,256]{1,0:T(8,128)S(1)}, f32[2304,256]{1,0:T(8,128)}, u32[]{:S(2)}) copy-start(f32[2304,256]{1,0:T(8,128)} %param.7) | copy-start | bytes 7077892
  53.1 11.6 %collective-permute-start.6 = (f32[16,2304]{1,0:T(8,128)S(1)}, f32[16,2304]{1,0:T(8,128)S(1)}, u32[]{:S(2)}, u32[]{:S(2)}) collective-permute-start(f32[16,2304]{1,0:T(8,128)S(1)} %dynamic-slice_bitcast_fusion.9), channel_id=1, source_target_pairs={{0,4},{2,6},{4,0},{6,2},{1,5},{3,7},{5,1},{7,3},{8,12},{10,14},{12... | collective-permute-start | bytes 442376 | tf_op jit(solution)/shard_map/ppermute | solution.py:78
  55.8 8.9 %collective-permute-start.8 = (f32[16,2304]{1,0:T(8,128)S(1)}, f32[16,2304]{1,0:T(8,128)S(1)}, u32[]{:S(2)}, u32[]{:S(2)}) collective-permute-start(f32[16,2304]{1,0:T(8,128)S(1)} %dynamic-slice_bitcast_fusion.8), channel_id=1, source_target_pairs={{0,1},{1,0},{2,3},{3,2},{4,5},{5,4},{6,7},{7,6},{8,9},{9,8},{10,11... | collective-permute-start | bytes 442376 | tf_op jit(solution)/shard_map/ppermute | solution.py:79
  59.4 8.1 %collective-permute-start.14 = (f32[16,2304]{1,0:T(8,128)S(1)}, f32[16,2304]{1,0:T(8,128)S(1)}, u32[]{:S(2)}, u32[]{:S(2)}) collective-permute-start(f32[16,2304]{1,0:T(8,128)S(1)} %dynamic-slice_bitcast_fusion.7), channel_id=1, source_target_pairs={{0,4},{2,6},{4,0},{6,2},{1,5},{3,7},{5,1},{7,3},{8,12},{10,14},{12... | collective-permute-start | bytes 442376 | tf_op jit(solution)/shard_map/ppermute | solution.py:78
  62.8 7.3 %collective-permute-start.16 = (f32[16,2304]{1,0:T(8,128)}, f32[16,2304]{1,0:T(8,128)}, u32[]{:S(2)}, u32[]{:S(2)}) collective-permute-start(f32[16,2304]{1,0:T(8,128)} %dynamic-slice_bitcast_fusion.6), channel_id=1, source_target_pairs={{0,1},{1,0},{2,3},{3,2},{4,5},{5,4},{6,7},{7,6},{8,9},{9,8},{10,11... | collective-permute-start | bytes 442376 | tf_op jit(solution)/shard_map/ppermute | solution.py:79
  74.5 12.7 %collective-permute-start.17 = (f32[32,576]{1,0:T(8,128)S(1)}, f32[32,576]{1,0:T(8,128)S(1)}, u32[]{:S(2)}, u32[]{:S(2)}) collective-permute-start(f32[32,576]{1,0:T(8,128)S(1)} %bitcast.157), channel_id=1, source_target_pairs={{0,8},{8,0},{16,24},{24,16},{1,9},{9,1},{17,25},{25,17},{2,10},{10... | collective-permute-start | bytes 221192 | tf_op jit(solution)/shard_map/ppermute | solution.py:86
  75.5 12.2 %collective-permute-start.18 = (f32[32,576]{1,0:T(8,128)S(1)}, f32[32,576]{1,0:T(8,128)S(1)}, u32[]{:S(2)}, u32[]{:S(2)}) collective-permute-start(f32[32,576]{1,0:T(8,128)S(1)} %bitcast.155), channel_id=1, source_target_pairs={{0,16},{8,24},{16,0},{24,8},{1,17},{9,25},{17,1},{25,9},{2,18},{10... | collective-permute-start | bytes 221192 | tf_op jit(solution)/shard_map/ppermute | solution.py:86
  78.0 9.7 %collective-permute-start.19 = (f32[32,576]{1,0:T(8,128)S(1)}, f32[32,576]{1,0:T(8,128)S(1)}, u32[]{:S(2)}, u32[]{:S(2)}) collective-permute-start(f32[32,576]{1,0:T(8,128)S(1)} %bitcast.158), channel_id=1, source_target_pairs={{0,24},{8,16},{16,8},{24,0},{1,25},{9,17},{17,9},{25,1},{2,26},{10... | collective-permute-start | bytes 221192 | tf_op jit(solution)/shard_map/ppermute | solution.py:86
  84.1 8.5 %collective-permute-start.10 = (f32[32,576]{1,0:T(8,128)S(1)}, f32[32,576]{1,0:T(8,128)S(1)}, u32[]{:S(2)}, u32[]{:S(2)}) collective-permute-start(f32[32,576]{1,0:T(8,128)S(1)} %bitcast.156), channel_id=1, source_target_pairs={{0,16},{8,24},{16,0},{24,8},{1,17},{9,25},{17,1},{25,9},{2,18},{10... | collective-permute-start | bytes 221192 | tf_op jit(solution)/shard_map/ppermute | solution.py:86
  84.8 7.8 %collective-permute-start.11 = (f32[32,576]{1,0:T(8,128)S(1)}, f32[32,576]{1,0:T(8,128)S(1)}, u32[]{:S(2)}, u32[]{:S(2)}) collective-permute-start(f32[32,576]{1,0:T(8,128)S(1)} %bitcast.159), channel_id=1, source_target_pairs={{0,24},{8,16},{16,8},{24,0},{1,25},{9,17},{17,9},{25,1},{2,26},{10... | collective-permute-start | bytes 221192 | tf_op jit(solution)/shard_map/ppermute | solution.py:86
  87.1 5.7 %collective-permute-start.9 = (f32[32,576]{1,0:T(8,128)S(1)}, f32[32,576]{1,0:T(8,128)S(1)}, u32[]{:S(2)}, u32[]{:S(2)}) collective-permute-start(f32[32,576]{1,0:T(8,128)S(1)} %bitcast.160), channel_id=1, source_target_pairs={{0,8},{8,0},{16,24},{24,16},{1,9},{9,1},{17,25},{25,17},{2,10},{10... | collective-permute-start | bytes 221192 | tf_op jit(solution)/shard_map/ppermute | solution.py:86
where the time goes:
time: 94 us; the launch traced here: 93.5 us
  starting transfers between devices  30.3 us (32%)
  matrix products  19.1 us (20%)
  waiting for transfers between devices  18.8 us (20%)
  local copies, waits for them, and re-layouts  12.7 us (14%)
  other arithmetic  11.1 us (12%)
  between operations  1.36 us (1%)
    dot_general x4, matrix products, matmul(): jnp.dot(taps, weights, precision=HIGH, preferred_element_type=jnp.float32)  13.9 us
    ppermute x6, starting transfers between devices, scatter_sum(): lax.ppermute(pick(blocks, here_lon ^ step, 0), 'lon', xor_perm(lon, step))  8.03 us
    ppermute x2, waiting for transfers between devices, scatter_sum(): got_0 = lax.ppermute(pick(ahead, 1 - y, 1), 'rep', xor_perm(rep, 1))  6.53 us
    ppermute x2, starting transfers between devices, scatter_sum(): got_0 = lax.ppermute(pick(sum_0, 1 - x, 0), 'lat', xor_perm(lat, 2))  5.39 us
    dot_general x2, matrix products, kernel_grad_t(): jnp.einsum('rd,rk->dk', grad_out, taps, precision=HIGH, preferred_element...  5.23 us
    transpose x2, local copies, waits for them, and re-layouts, transpose_kernel(): return jnp.swapaxes(stacked, 1, 2).reshape(9 * channels, channels)  5.14 us
    ppermute x2, starting transfers between devices, halo(): lax.ppermute(lax.slice_in_dim(block, size - width, size, axis=dim), axis,...  4.81 us
    ppermute x6, waiting for transfers between devices, scatter_sum(): lax.ppermute(pick(blocks, here_lon ^ step, 0), 'lon', xor_perm(lon, step))  4.48 us
  transfers between devices with their start and end apart: 20, of which 8 were waited for; matrix products, arithmetic and copies ran while one was open for 23% of the time, Pallas kernels for 0%

commit v1 on v0

v1 whole, which is shorter than its diff:
```python
import math

import jax
import jax.numpy as jnp
from jax import lax
from jax.sharding import PartitionSpec as P

HIGH = lax.Precision.HIGH


def shift_perm(count, periodic):
    forward = [(i, i + 1) for i in range(count - 1)]
    if periodic:
        forward.append((count - 1, 0))
    return forward, [(b, a) for a, b in forward]


def pair_swap(block_low, block_high, axis):
    count = lax.axis_size(axis)
    even = lax.axis_index(axis) % 2 == 0
    pairs = [(i, i + 1) for i in range(0, count - 1, 2)]
    mates = [(i, i + 1) for i in range(1, count - 1, 2)]

    def swap(block, who):
        return lax.ppermute(block, axis, who + [(b, a) for a, b in who])

    one = swap(jnp.where(even, block_high, block_low), pairs)
    two = swap(jnp.where(even, block_low, block_high), mates)
    return jnp.where(even, two, one), jnp.where(even, one, two)


def extend(field, width):
    rows, cols, channels = field.shape
    low, high = pair_swap(field[:width], field[rows - width :], "lat")
    forward, backward = shift_perm(lax.axis_size("lon"), True)
    left = lax.ppermute(jnp.swapaxes(field[:, cols - width :], 0, 1), "lon", forward)
    right = lax.ppermute(jnp.swapaxes(field[:, :width], 0, 1), "lon", backward)
    edge = jnp.concatenate([low, high], axis=0)
    corner_left = lax.ppermute(
        edge[:, cols - width :].reshape(-1, channels), "lon", forward
    ).reshape(2, width, width, channels)
    corner_right = lax.ppermute(edge[:, :width].reshape(-1, channels), "lon", backward).reshape(
        2, width, width, channels
    )
    left, right = jnp.swapaxes(left, 0, 1), jnp.swapaxes(right, 0, 1)
    return jnp.concatenate(
        [
            jnp.concatenate([corner_left[0], low, corner_right[0]], axis=1),
            jnp.concatenate([left, field, right], axis=1),
            jnp.concatenate([corner_left[1], high, corner_right[1]], axis=1),
        ],
        axis=0,
    )


def taps_of(padded, rows, cols, flipped):
    pieces = []
    for a in range(3):
        for b in range(3):
            r, c = (2 - a, 2 - b) if flipped else (a, b)
            pieces.append(padded[r : r + rows, c : c + cols, :])
    return jnp.concatenate(pieces, axis=-1).reshape(rows * cols, -1)


def matmul(taps, weights):
    return jnp.dot(taps, weights, precision=HIGH, preferred_element_type=jnp.float32)


def transpose_kernel(weights):
    channels = weights.shape[1]
    stacked = weights.reshape(9, channels, channels)
    return jnp.swapaxes(stacked, 1, 2).reshape(9 * channels, channels)


def silu_slope(value):
    sigma = jax.nn.sigmoid(value)
    return sigma * (1.0 + value * (1.0 - sigma))


def kernel_grad_t(taps, grad_out, order):
    rows, channels = grad_out.shape
    blocks = grad_out.T.reshape(8, channels // 8, rows)
    grad_t = jnp.concatenate(
        [lax.dynamic_index_in_dim(blocks, i, 0, keepdims=False) for i in order], axis=0
    )
    return jnp.einsum(
        "dr,rk->dk", grad_t, taps, precision=HIGH, preferred_element_type=jnp.float32
    )


def plane_perm(count, even, odd):
    return [(i, i ^ (odd if (i // 2) % 2 else even)) for i in range(count)]


def relative_blocks(flip):
    lat, y = lax.axis_index("lat"), lax.axis_index("rep")
    x, core = lat // 2, lat % 2
    order = []
    for r_core in range(2):
        c = core ^ r_core
        y_first = (c == 0) != flip
        for r_first in range(2):
            for r_second in range(2):
                there_y = y ^ jnp.where(y_first, r_first, r_second)
                there_x = x ^ jnp.where(y_first, r_second, r_first)
                order.append(there_x * 4 + c * 2 + there_y)
    return order


def scatter_sum(part, flip):
    channels, taps = part.shape
    lon, lat, rep = lax.axis_size("lon"), lax.axis_size("lat"), lax.axis_size("rep")
    plane = lat * rep
    each = channels // plane
    one, two = (4, 1) if flip else (1, 4)
    view = part.reshape(2, 2, 2, each, taps)
    held = view[0] + lax.ppermute(view[1], ("lat", "rep"), plane_perm(plane, 2, 2))
    held = held[0] + lax.ppermute(held[1], ("lat", "rep"), plane_perm(plane, one, two))
    tail = held[0] + lax.ppermute(held[1], ("lat", "rep"), plane_perm(plane, two, one))
    if lon != 4:
        return lax.psum_scatter(tail, "lon", scatter_dimension=1, tiled=True).T
    blocks = jnp.swapaxes(tail.reshape(each, lon, taps // lon), 0, 1)
    z = lax.axis_index("lon")
    low_first = (lax.axis_index("lat") % 2 == 0) != flip
    ordered = []
    for r_first in range(2):
        for r_second in range(2):
            step = jnp.where(low_first, r_first + 2 * r_second, 2 * r_first + r_second)
            ordered.append(lax.dynamic_index_in_dim(blocks, z ^ step, 0, keepdims=False))
    blocks = jnp.stack(ordered).reshape(2, 2, each, taps // lon)
    axes = ("lon", "lat")
    low, high = (2, 1) if flip else (1, 2)

    def lane(even, odd):
        return [(i, i ^ (lat * (odd if i % 2 else even))) for i in range(lon * lat)]

    held = blocks[0] + lax.ppermute(blocks[1], axes, lane(low, high))
    return (held[0] + lax.ppermute(held[1], axes, lane(high, low))).T


def local(inputs, cotangent, first_weight, second_weight):
    channels = inputs.shape[3]
    rows, cols = inputs.shape[1], inputs.shape[2]
    here = inputs[0]
    grad = cotangent[0]
    first_back = transpose_kernel(first_weight)
    second_back = transpose_kernel(second_weight)
    wide_in, wide_cot = extend(here, 2), extend(grad, 2)
    row = lax.axis_index("lat") * rows - 1 + jnp.arange(rows + 2)
    inside = ((row >= 0) & (row < rows * lax.axis_size("lat")))[:, None, None]
    er, ec = rows + 2, cols + 2
    act_in = jax.nn.silu(wide_in)
    hidden = matmul(taps_of(act_in, er, ec, False), first_weight).reshape(er, ec, channels)
    act_hidden = jnp.where(inside, jax.nn.silu(hidden), 0.0)
    second_taps = taps_of(act_hidden, rows, cols, False)
    scale = 1.0 / math.sqrt(
        rows * cols * lax.axis_size("rep") * lax.axis_size("lat") * lax.axis_size("lon")
    )
    second_part = kernel_grad_t(second_taps, grad.reshape(rows * cols, channels), relative_blocks(False)) * scale
    second_grad = scatter_sum(second_part, False)
    hidden_grad = matmul(taps_of(wide_cot, er, ec, True), second_back).reshape(er, ec, channels)
    hidden_grad = jnp.where(inside, hidden_grad * silu_slope(hidden), 0.0)
    first_taps = taps_of(act_in[1:-1, 1:-1], rows, cols, False)
    first_part = (
        kernel_grad_t(first_taps, hidden_grad[1:-1, 1:-1].reshape(rows * cols, channels), relative_blocks(True)) * scale
    )
    first_grad = scatter_sum(first_part, True)
    output = inputs + matmul(second_taps, second_weight).reshape(inputs.shape)
    back = matmul(taps_of(hidden_grad, rows, cols, True), first_back).reshape(inputs.shape)
    input_grad = cotangent + back * silu_slope(inputs)
    return (output, input_grad, first_grad, second_grad)


def solution(mesh):
    in_specs = (P("rep", "lat", "lon", None), P("rep", "lat", "lon", None), P(), P())
    out_specs = (
        P("rep", "lat", "lon", None),
        P("rep", "lat", "lon", None),
        P("lon", ("lat", "rep")),
        P("lon", ("lat", "rep")),
    )
    return jax.shard_map(local, mesh=mesh, in_specs=in_specs, out_specs=out_specs, check_vma=False)
```

time: 94 us -> 122 us (1.30)
  waiting for transfers between devices: 18.8 us -> 46.8 us
  local copies, waits for them, and re-layouts: 12.7 us -> 23.6 us
  starting transfers between devices: 30.3 us -> 24.4 us
  other arithmetic: 11.1 us -> 5.35 us
    ppermute x20 -> x22, waiting for transfers between devices: 18.8 us -> 46.8 us  [the longest x2 12.9 us: scatter_sum(): lax.ppermute(held[1], ('lat', 'rep'), plane_perm(plane, one, two))]
    unnamed x60 -> x82, local copies, waits for them, and re-layouts: 3.14 us -> 10.9 us
    ppermute x20 -> x22, starting transfers between devices: 30.3 us -> 24.4 us  [the longest x4 7.03 us: swap(): return lax.ppermute(block, axis, who + [(b, a) for a, b in who])]
    concatenate x4 -> x2, other arithmetic: 4.92 us -> 0.24 us  [extend(): jnp.concatenate([jnp.concatenate([corner_left[0], low, corner_right[0]],...]
    transpose x0 -> x3, local copies, waits for them, and re-layouts: none -> 3.6 us  [the longest x2 2.6 us: extend(): jnp.swapaxes(field[:, cols - width:], 0, 1)]
    slice x2, other arithmetic: 2.64 us -> 0.02 us  [extend(): edge[:, cols - width:].reshape(-1, channels)]
    select_n x0 -> x4, other arithmetic: none -> 1.94 us  [the longest x2 1.92 us: pair_swap(): two = swap(jnp.where(even, block_low, block_high), mates)]
    reshape x2, local copies, waits for them, and re-layouts: 2.42 us -> 0.52 us  [scatter_sum(): blocks = jnp.swapaxes(tail.reshape(each, lon, taps // lon), 0, 1)]
  transfers between devices with their start and end apart: 20 -> 22, of which waited for: 8 -> 10; matrix products, arithmetic and copies ran while one was open for 23% -> 23% of each run, Pallas kernels for 0% -> 0%
where the time goes in v1:
time: 122 us; the launch traced here: 121 us
  waiting for transfers between devices  46.8 us (38%)
  starting transfers between devices  24.4 us (20%)
  local copies, waits for them, and re-layouts  23.6 us (19%)
  matrix products  19.4 us (16%)
  other arithmetic  5.35 us (4%)
  between operations  1.69 us (1%)
    dot_general x4, matrix products, matmul(): jnp.dot(taps, weights, precision=HIGH, preferred_element_type=jnp.float32)  14 us
    ppermute x2, waiting for transfers between devices, scatter_sum(): lax.ppermute(held[1], ('lat', 'rep'), plane_perm(plane, one, two))  12.9 us
    unnamed x82, local copies, waits for them, and re-layouts  10.9 us
    ppermute x2, waiting for transfers between devices, extend(): lax.ppermute(edge[:, cols - width:].reshape(-1, channels), 'lon', forward)  10.8 us
    ppermute x2, waiting for transfers between devices, extend(): lax.ppermute(edge[:, :width].reshape(-1, channels), 'lon', backward)  7.07 us
    ppermute x4, starting transfers between devices, swap(): return lax.ppermute(block, axis, who + [(b, a) for a, b in who])  7.03 us
    ppermute x2, waiting for transfers between devices, scatter_sum(): held = blocks[0] + lax.ppermute(blocks[1], axes, lane(low, high))  6.61 us
    ppermute x2, starting transfers between devices, extend(): right = lax.ppermute(jnp.swapaxes(field[:, :width], 0, 1), 'lon', backward)  6.12 us
  transfers between devices with their start and end apart: 22, of which 10 were waited for; matrix products, arithmetic and copies ran while one was open for 23% of the time, Pallas kernels for 0%

profile of v1, /device:TPU:0, one launch (start us, length us, event | category | flops | bytes accessed | tf_op | source)
XLA Modules:
  0.0 121.1 jit_solution(11159336563023472863)
XLA Ops:
  0.7 1.0 select_bitcast_fusion.1
  1.7 0.7 collective-permute-start.8
  2.4 4.4 %collective-permute-start.9 = (f32[2,32,256]{2,1,0:T(8,128)S(1)}, f32[2,32,256]{2,1,0:T(8,128)S(1)}, u32[]{:S(2)}, u32[]{:S(2)}) collective-permute-start(f32[2,32,256]{2,1,0:T(8,128)S(1)} %get-tuple-element.15), channel_id=1, source_target_pairs={{0,2},{4,6},{2,0},{6,4},{1,3},{5,7},{3,1},{7,5},{8,10},{12,14},{10... | collective-permute-start | bytes 196616 | tf_op jit(solution)/shard_map/ppermute | solution.py:25
  6.7 1.0 slice_bitcast_fusion.13
  7.7 1.6 %collective-permute-start.6 = (f32[2,16,256]{2,0,1:T(2,128)S(1)}, f32[2,16,256]{2,0,1:T(2,128)S(1)}, u32[]{:S(2)}, u32[]{:S(2)}) collective-permute-start(f32[2,16,256]{2,0,1:T(2,128)S(1)} %get-tuple-element.12), channel_id=1, source_target_pairs={{0,8},{8,16},{16,24},{24,0},{1,9},{9,17},{17,25},{25,1},{2,10},{10... | collective-permute-start | bytes 98312 | tf_op jit(solution)/shard_map/ppermute | solution.py:36
  9.4 2.2 %collective-permute-start.7 = (f32[2,16,256]{2,0,1:T(2,128)S(1)}, f32[2,16,256]{2,0,1:T(2,128)S(1)}, u32[]{:S(2)}, u32[]{:S(2)}) collective-permute-start(f32[2,16,256]{2,0,1:T(2,128)S(1)} %get-tuple-element.13), channel_id=1, source_target_pairs={{8,0},{16,8},{24,16},{0,24},{9,1},{17,9},{25,17},{1,25},{10,2},{18... | collective-permute-start | bytes 98312 | tf_op jit(solution)/shard_map/ppermute | solution.py:37
  11.6 0.9 select_bitcast_fusion.3
  12.5 0.7 collective-permute-start
  13.3 1.6 %slice_bitcast_fusion.15 = (f32[2,16,256]{2,0,1:T(2,128)}, f32[2,16,256]{2,0,1:T(2,128)S(1)}) fusion(f32[16,32,256]{2,1,0:T(8,128)} %bitcast.189), kind=kLoop, calls=%fused_computation.120 | loop fusion | bytes 131072 | tf_op jit(solution)/shard_map/transpose | solution.py:36
  14.9 3.1 %copy.30 = f32[9,256,256]{2,1,0:T(8,128)} copy(f32[9,256,256]{1,2,0:T(8,128)} %bitcast.186) | data formatting | bytes 4718592 | tf_op jit(solution)/shard_map/transpose | solution.py:72
  18.0 1.0 copy.37
  19.0 1.9 %copy.31 = f32[9,256,256]{2,1,0:T(8,128)} copy(f32[9,256,256]{1,2,0:T(8,128)S(1)} %bitcast.185) | data formatting | bytes 4718592 | tf_op jit(solution)/shard_map/transpose | solution.py:72
  20.9 1.3 %collective-permute-start.1 = (f32[2,32,256]{2,1,0:T(8,128)S(1)}, f32[2,32,256]{2,1,0:T(8,128)S(1)}, u32[]{:S(2)}, u32[]{:S(2)}) collective-permute-start(f32[2,32,256]{2,1,0:T(8,128)S(1)} %get-tuple-element.19), channel_id=1, source_target_pairs={{0,2},{4,6},{2,0},{6,4},{1,3},{5,7},{3,1},{7,5},{8,10},{12,14},{10... | collective-permute-start | bytes 196616 | tf_op jit(solution)/shard_map/ppermute | solution.py:25
  22.3 3.9 %collective-permute-start.5 = (f32[2,16,256]{2,0,1:T(2,128)S(1)}, f32[2,16,256]{2,0,1:T(2,128)S(1)}, u32[]{:S(2)}, u32[]{:S(2)}) collective-permute-start(f32[2,16,256]{2,0,1:T(2,128)S(1)} %get-tuple-element.17), channel_id=1, source_target_pairs={{8,0},{16,8},{24,16},{0,24},{9,1},{17,9},{25,17},{1,25},{10,2},{18... | collective-permute-start | bytes 98312 | tf_op jit(solution)/shard_map/ppermute | solution.py:37
  26.3 5.4 %collective-permute-done.10 = f32[8,256]{1,0:T(8,128)S(1)} collective-permute-done((f32[8,256]{1,0:T(8,128)S(1)}, f32[8,256]{1,0:T(8,128)S(1)}, u32[]{:S(2)}, u32[]{:S(2)}) %collective-permute-start.10) | collective-permute-done | bytes 8224 | tf_op jit(solution)/shard_map/ppermute | solution.py:39
  31.7 3.6 %collective-permute-done.11 = f32[8,256]{1,0:T(8,128)S(1)} collective-permute-done((f32[8,256]{1,0:T(8,128)S(1)}, f32[8,256]{1,0:T(8,128)S(1)}, u32[]{:S(2)}, u32[]{:S(2)}) %collective-permute-start.11) | collective-permute-done | bytes 8224 | tf_op jit(solution)/shard_map/ppermute | solution.py:42
  35.3 5.4 %collective-permute-done.2 = f32[8,256]{1,0:T(8,128)S(1)} collective-permute-done((f32[8,256]{1,0:T(8,128)S(1)}, f32[8,256]{1,0:T(8,128)S(1)}, u32[]{:S(2)}, u32[]{:S(2)}) %collective-permute-start.2) | collective-permute-done | bytes 8224 | tf_op jit(solution)/shard_map/ppermute | solution.py:39
  40.9 0.1 maximum_maximum_fusion.3
  41.0 3.4 %collective-permute-done.3 = f32[8,256]{1,0:T(8,128)S(1)} collective-permute-done((f32[8,256]{1,0:T(8,128)S(1)}, f32[8,256]{1,0:T(8,128)S(1)}, u32[]{:S(2)}, u32[]{:S(2)}) %collective-permute-start.3) | collective-permute-done | bytes 8224 | tf_op jit(solution)/shard_map/ppermute | solution.py:42
  44.4 0.1 maximum_maximum_fusion.1
  44.6 1.3 %divide_multiply_fusion = f32[20,36,256]{2,1,0:T(8,128)S(1)} fusion(f32[2,2,256]{2,1,0:T(2,128)S(1)} %squeeze.144, f32[2,32,256]{2,1,0:T(8,128)S(1)} %get-tuple-element.35, f32[2,2,256]{2,1,0:T(2,128)S(1)} %squeeze.143, f32[16,2,256]{2,1,0:T(2,128)S(1)} %bitcast.228, f32[16,32,256]{2,1,0:T(8,128)} %bitcast.190, f32[16,2,256]{2,1,0:T(2,128)S(1)} %bitcast.227, ...), kind=kLoop, calls=%fused_computation.15 | loop fusion | flops 2211840 | bytes 1474560 | tf_op jit(solution)/shard_map/jit(silu)/mul | solution.py:152
  46.0 0.9 slice_dynamic-update-slice_fusion.26
  47.9 1.3 %copy-done.3 = f32[2304,256]{1,0:T(8,128)S(1)} copy-done((f32[2304,256]{1,0:T(8,128)S(1)}, f32[2304,256]{1,0:T(8,128)}, u32[]{:S(2)}) %copy-start.3) | copy-done | bytes 2359320
  49.2 2.9 %multiply_select_fusion = (f32[18,34,256]{2,1,0:T(8,128)S(1)}, f32[18,34,256]{2,1,0:T(8,128)S(1)}) fusion(pred[18]{0:T(512)(128)(4,1)S(1)} %compare_and_fusion, f32[18,34,2304]{2,1,0:T(8,128)S(1)} %slice_dynamic-update-slice_fusion.9, f32[2304,256]{1,0:T(8,128)S(1)} %copy-done.3), kind=kOutput, calls=%fused_computation.36 | convolution fusion | flops 2166617088 | bytes 9252882 | tf_op jit(solution)/shard_map/dot_general | solution.py:66
  52.1 2.9 %fusion.4 = f32[18,34,256]{2,1,0:T(8,128)S(1)} fusion(f32[18,34,2304]{2,1,0:T(8,128)S(1)} %slice_dynamic-update-slice_fusion, f32[2304,256,1]{1,0,2:T(8,128)S(1)} %bitcast.188, f32[18,34,256]{2,1,0:T(8,128)S(1)} %get-tuple-element.45, pred[18]{0:T(512)(128)(4,1)S(1)} %compare_and_fusion), kind=kOutput, calls=%fused_computation.7 | convolution fusion | flops 2167243776 | bytes 9252882 | tf_op jit(solution)/shard_map/dot_general | solution.py:66
  55.0 0.9 slice_dynamic-update-slice_fusion.34
  55.9 0.9 slice_dynamic-update-slice_fusion.33
  56.9 0.9 slice_dynamic-update-slice_fusion.32
  57.8 0.9 slice_dynamic-update-slice_fusion.31
  58.7 1.0 fusion.23
  59.6 0.2 copy.32
  60.4 0.5 copy-done.8
  61.1 2.6 %convolution_multiply_fusion = f32[256,2304]{1,0:T(8,128)S(1)} fusion(f32[256,512]{1,0:T(8,128)S(1)} %constant_dynamic-update-slice_fusion.9, f32[512,2304]{1,0:T(8,128)S(1)} %bitcast.180), kind=kOutput, calls=%fused_computation | convolution fusion | flops 1812529152 | bytes 7602176 | tf_op jit(solution)/shard_map/dr,rk->dk/dot_general | solution.py:86
  63.7 0.2 fusion.21
  64.6 2.8 %convolution_multiply_fusion.1 = f32[256,2304]{1,0:T(8,128)S(1)} fusion(f32[256,512]{1,0:T(8,128)S(1)} %constant_dynamic-update-slice_fusion.1, f32[512,2304]{1,0:T(8,128)S(1)} %bitcast.193), kind=kOutput, calls=%fused_computation.1 | convolution fusion | flops 1812529152 | bytes 7602176 | tf_op jit(solution)/shard_map/dr,rk->dk/dot_general | solution.py:86
  67.4 0.2 fusion.22
  67.6 0.5 collective-permute-start.12
  68.1 0.9 slice_dynamic-update-slice_fusion.30
  69.0 0.9 slice_dynamic-update-slice_fusion.29
  69.9 0.9 slice_dynamic-update-slice_fusion.28
  70.8 2.9 %fusion.10 = f32[1,16,32,256]{3,2,1,0:T(8,128)} fusion(f32[1,16,32,256]{3,2,1,0:T(8,128)S(1)} %copy-done.7, f32[16,32,2304]{2,1,0:T(8,128)S(1)} %slice_dynamic-update-slice_fusion.35, f32[2304,256]{1,0:T(8,128)S(1)} %copy-done.4), kind=kOutput, calls=%fused_computation.12 | convolution fusion | flops 1812070400 | bytes 8126464 | tf_op jit(solution)/shard_map/dot_general | solution.py:66
  73.7 0.9 slice_dynamic-update-slice_fusion.27
  74.6 5.3 %fusion.9 = f32[1,16,32,256]{3,2,1,0:T(8,128)} fusion(f32[1,16,32,256]{3,2,1,0:T(8,128)S(1)} %copy-done.1, f32[16,32,2304]{2,1,0:T(8,128)} %slice_dynamic-update-slice_fusion.27, f32[2304,256,1]{1,0,2:T(8,128)S(1)} %bitcast.187, f32[1,16,32,256]{3,2,1,0:T(8,128)S(1)} %copy-done.7), kind=kOutput, calls=%fused_computation.11 | convolution fusion | flops 1813118976 | bytes 8650752 | tf_op jit(solution)/shard_map/dot_general | solution.py:66
  80.0 0.2 add.272
  80.2 1.6 %collective-permute-start.18 = (f32[2,32,2304]{2,1,0:T(8,128)S(1)}, f32[2,32,2304]{2,1,0:T(8,128)S(1)}, u32[]{:S(2)}, u32[]{:S(2)}) collective-permute-start(f32[2,32,2304]{2,1,0:T(8,128)S(1)} %slice_bitcast_fusion), channel_id=1, source_target_pairs={{0,1},{1,0},{2,6},{3,7},{4,5},{5,4},{6,2},{7,3},{8,9},{9,8},{10,14... | collective-permute-start | bytes 1769480 | tf_op jit(solution)/shard_map/ppermute | solution.py:118
  81.7 0.1 add.251
  81.9 1.3 %collective-permute-start.13 = (f32[2,32,2304]{2,1,0:T(8,128)S(1)}, f32[2,32,2304]{2,1,0:T(8,128)S(1)}, u32[]{:S(2)}, u32[]{:S(2)}) collective-permute-start(f32[2,32,2304]{2,1,0:T(8,128)S(1)} %slice_bitcast_fusion.2), channel_id=1, source_target_pairs={{0,4},{1,5},{2,3},{3,2},{4,0},{5,1},{6,7},{7,6},{8,12},{9,13},{10,... | collective-permute-start | bytes 1769480 | tf_op jit(solution)/shard_map/ppermute | solution.py:118
  83.2 12.9 %collective-permute-done.18 = f32[2,32,2304]{2,1,0:T(8,128)S(1)} collective-permute-done((f32[2,32,2304]{2,1,0:T(8,128)S(1)}, f32[2,32,2304]{2,1,0:T(8,128)S(1)}, u32[]{:S(2)}, u32[]{:S(2)}) %collective-permute-start.18) | collective-permute-done | bytes 589856 | tf_op jit(solution)/shard_map/ppermute | solution.py:118
  96.2 1.4 %collective-permute-start.19 = (f32[32,2304]{1,0:T(8,128)S(1)}, f32[32,2304]{1,0:T(8,128)S(1)}, u32[]{:S(2)}, u32[]{:S(2)}) collective-permute-start(f32[32,2304]{1,0:T(8,128)S(1)} %slice_bitcast_fusion.4), channel_id=1, source_target_pairs={{0,4},{1,5},{2,3},{3,2},{4,0},{5,1},{6,7},{7,6},{8,12},{9,13},{10,... | collective-permute-start | bytes 884744 | tf_op jit(solution)/shard_map/ppermute | solution.py:119
  97.7 0.1 fusion.14
  97.8 1.6 %collective-permute-start.14 = (f32[32,2304]{1,0:T(8,128)S(1)}, f32[32,2304]{1,0:T(8,128)S(1)}, u32[]{:S(2)}, u32[]{:S(2)}) collective-permute-start(f32[32,2304]{1,0:T(8,128)S(1)} %slice_bitcast_fusion.6), channel_id=1, source_target_pairs={{0,1},{1,0},{2,6},{3,7},{4,5},{5,4},{6,2},{7,3},{8,9},{9,8},{10,14... | collective-permute-start | bytes 884744 | tf_op jit(solution)/shard_map/ppermute | solution.py:119
  99.4 6.0 %collective-permute-done.19 = f32[32,2304]{1,0:T(8,128)S(1)} collective-permute-done((f32[32,2304]{1,0:T(8,128)S(1)}, f32[32,2304]{1,0:T(8,128)S(1)}, u32[]{:S(2)}, u32[]{:S(2)}) %collective-permute-start.19) | collective-permute-done | bytes 294944 | tf_op jit(solution)/shard_map/ppermute | solution.py:119
  105.4 0.3 reshape.155
  105.6 0.3 constant_dynamic-slice_fusion.3
  106.1 0.3 reshape.152
  106.4 0.3 constant_dynamic-slice_fusion.7
  106.8 2.4 %collective-permute-start.15 = (f32[2,32,576]{2,1,0:T(8,128)S(1)}, f32[2,32,576]{2,1,0:T(8,128)S(1)}, u32[]{:S(2)}, u32[]{:S(2)}) collective-permute-start(f32[2,32,576]{2,1,0:T(8,128)S(1)} %pad_maximum_fusion), channel_id=1, source_target_pairs={{0,16},{2,10},{4,20},{6,14},{8,24},{10,2},{12,28},{14,6},{16,0},{1... | collective-permute-start | bytes 442376 | tf_op jit(solution)/shard_map/ppermute | solution.py:137
  109.2 4.7 %collective-permute-done.20 = f32[2,32,576]{2,1,0:T(8,128)S(1)} collective-permute-done((f32[2,32,576]{2,1,0:T(8,128)S(1)}, f32[2,32,576]{2,1,0:T(8,128)S(1)}, u32[]{:S(2)}, u32[]{:S(2)}) %collective-permute-start.20) | collective-permute-done | bytes 147488 | tf_op jit(solution)/shard_map/ppermute | solution.py:137
  114.0 1.9 %collective-permute-done.15 = f32[2,32,576]{2,1,0:T(8,128)S(1)} collective-permute-done((f32[2,32,576]{2,1,0:T(8,128)S(1)}, f32[2,32,576]{2,1,0:T(8,128)S(1)}, u32[]{:S(2)}, u32[]{:S(2)}) %collective-permute-start.15) | collective-permute-done | bytes 147488 | tf_op jit(solution)/shard_map/ppermute | solution.py:137
  116.0 0.5 collective-permute-start.16
  116.5 2.8 %collective-permute-done.21 = f32[32,576]{1,0:T(8,128)S(1)} collective-permute-done((f32[32,576]{1,0:T(8,128)S(1)}, f32[32,576]{1,0:T(8,128)S(1)}, u32[]{:S(2)}, u32[]{:S(2)}) %collective-permute-start.21) | collective-permute-done | bytes 73760 | tf_op jit(solution)/shard_map/ppermute | solution.py:138
  119.3 0.6 fusion.18
  120.0 0.5 collective-permute-done.16
  120.5 0.6 fusion.20
  (133 shorter events, 3.0 us)
Async XLA Ops:
  0.6 17.4 %copy-start = (f32[1,16,32,256]{3,2,1,0:T(8,128)S(1)}, f32[1,16,32,256]{3,2,1,0:T(8,128)}, u32[]{:S(2)}) copy-start(f32[1,16,32,256]{3,2,1,0:T(8,128)} %param.5) | copy-start | bytes 1572868
  0.6 18.3 %copy-start.2 = (f32[2304,256]{1,0:T(8,128)S(1)}, f32[2304,256]{1,0:T(8,128)}, u32[]{:S(2)}) copy-start(f32[2304,256]{1,0:T(8,128)} %param.6) | copy-start | bytes 7077892
  1.7 19.2 %collective-permute-start.8 = (f32[2,32,256]{2,1,0:T(8,128)S(1)}, f32[2,32,256]{2,1,0:T(8,128)S(1)}, u32[]{:S(2)}, u32[]{:S(2)}) collective-permute-start(f32[2,32,256]{2,1,0:T(8,128)S(1)} %get-tuple-element.14), channel_id=1, source_target_pairs={{2,4},{4,2},{3,5},{5,3},{10,12},{12,10},{11,13},{13,11},{18,20},{2... | collective-permute-start | bytes 196616 | tf_op jit(solution)/shard_map/ppermute | solution.py:25
  2.4 19.9 %collective-permute-start.9 = (f32[2,32,256]{2,1,0:T(8,128)S(1)}, f32[2,32,256]{2,1,0:T(8,128)S(1)}, u32[]{:S(2)}, u32[]{:S(2)}) collective-permute-start(f32[2,32,256]{2,1,0:T(8,128)S(1)} %get-tuple-element.15), channel_id=1, source_target_pairs={{0,2},{4,6},{2,0},{6,4},{1,3},{5,7},{3,1},{7,5},{8,10},{12,14},{10... | collective-permute-start | bytes 196616 | tf_op jit(solution)/shard_map/ppermute | solution.py:25
  7.7 33.1 %collective-permute-start.6 = (f32[2,16,256]{2,0,1:T(2,128)S(1)}, f32[2,16,256]{2,0,1:T(2,128)S(1)}, u32[]{:S(2)}, u32[]{:S(2)}) collective-permute-start(f32[2,16,256]{2,0,1:T(2,128)S(1)} %get-tuple-element.12), channel_id=1, source_target_pairs={{0,8},{8,16},{16,24},{24,0},{1,9},{9,17},{17,25},{25,1},{2,10},{10... | collective-permute-start | bytes 98312 | tf_op jit(solution)/shard_map/ppermute | solution.py:36
  9.4 31.5 %collective-permute-start.7 = (f32[2,16,256]{2,0,1:T(2,128)S(1)}, f32[2,16,256]{2,0,1:T(2,128)S(1)}, u32[]{:S(2)}, u32[]{:S(2)}) collective-permute-start(f32[2,16,256]{2,0,1:T(2,128)S(1)} %get-tuple-element.13), channel_id=1, source_target_pairs={{8,0},{16,8},{24,16},{0,24},{9,1},{17,9},{25,17},{1,25},{10,2},{18... | collective-permute-start | bytes 98312 | tf_op jit(solution)/shard_map/ppermute | solution.py:37
  12.5 9.8 %collective-permute-start = (f32[2,32,256]{2,1,0:T(8,128)S(1)}, f32[2,32,256]{2,1,0:T(8,128)S(1)}, u32[]{:S(2)}, u32[]{:S(2)}) collective-permute-start(f32[2,32,256]{2,1,0:T(8,128)S(1)} %get-tuple-element.18), channel_id=1, source_target_pairs={{2,4},{4,2},{3,5},{5,3},{10,12},{12,10},{11,13},{13,11},{18,20},{2... | collective-permute-start | bytes 196616 | tf_op jit(solution)/shard_map/ppermute | solution.py:25
  20.9 5.3 %collective-permute-start.1 = (f32[2,32,256]{2,1,0:T(8,128)S(1)}, f32[2,32,256]{2,1,0:T(8,128)S(1)}, u32[]{:S(2)}, u32[]{:S(2)}) collective-permute-start(f32[2,32,256]{2,1,0:T(8,128)S(1)} %get-tuple-element.19), channel_id=1, source_target_pairs={{0,2},{4,6},{2,0},{6,4},{1,3},{5,7},{3,1},{7,5},{8,10},{12,14},{10... | collective-permute-start | bytes 196616 | tf_op jit(solution)/shard_map/ppermute | solution.py:25
  22.3 22.3 %collective-permute-start.4 = (f32[2,16,256]{2,0,1:T(2,128)}, f32[2,16,256]{2,0,1:T(2,128)S(1)}, u32[]{:S(2)}, u32[]{:S(2)}) collective-permute-start(f32[2,16,256]{2,0,1:T(2,128)} %get-tuple-element.16), channel_id=1, source_target_pairs={{0,8},{8,16},{16,24},{24,0},{1,9},{9,17},{17,25},{25,1},{2,10},{10... | collective-permute-start | bytes 98312 | tf_op jit(solution)/shard_map/ppermute | solution.py:36
  22.3 22.3 %collective-permute-start.5 = (f32[2,16,256]{2,0,1:T(2,128)S(1)}, f32[2,16,256]{2,0,1:T(2,128)S(1)}, u32[]{:S(2)}, u32[]{:S(2)}) collective-permute-start(f32[2,16,256]{2,0,1:T(2,128)S(1)} %get-tuple-element.17), channel_id=1, source_target_pairs={{8,0},{16,8},{24,16},{0,24},{9,1},{17,9},{25,17},{1,25},{10,2},{18... | collective-permute-start | bytes 98312 | tf_op jit(solution)/shard_map/ppermute | solution.py:37
  26.2 5.4 %collective-permute-start.10 = (f32[8,256]{1,0:T(8,128)S(1)}, f32[8,256]{1,0:T(8,128)S(1)}, u32[]{:S(2)}, u32[]{:S(2)}) collective-permute-start(f32[8,256]{1,0:T(8,128)S(1)} %reshape.143), channel_id=1, source_target_pairs={{0,8},{8,16},{16,24},{24,0},{1,9},{9,17},{17,25},{25,1},{2,10},{10... | collective-permute-start | bytes 24584 | tf_op jit(solution)/shard_map/ppermute | solution.py:39
  31.7 3.7 %collective-permute-start.11 = (f32[8,256]{1,0:T(8,128)S(1)}, f32[8,256]{1,0:T(8,128)S(1)}, u32[]{:S(2)}, u32[]{:S(2)}) collective-permute-start(f32[8,256]{1,0:T(8,128)S(1)} %reshape.144), channel_id=1, source_target_pairs={{8,0},{16,8},{24,16},{0,24},{9,1},{17,9},{25,17},{1,25},{10,2},{18... | collective-permute-start | bytes 24584 | tf_op jit(solution)/shard_map/ppermute | solution.py:42
  35.3 5.4 %collective-permute-start.2 = (f32[8,256]{1,0:T(8,128)S(1)}, f32[8,256]{1,0:T(8,128)S(1)}, u32[]{:S(2)}, u32[]{:S(2)}) collective-permute-start(f32[8,256]{1,0:T(8,128)S(1)} %reshape.141), channel_id=1, source_target_pairs={{0,8},{8,16},{16,24},{24,0},{1,9},{9,17},{17,25},{25,1},{2,10},{10... | collective-permute-start | bytes 24584 | tf_op jit(solution)/shard_map/ppermute | solution.py:39
  40.8 3.7 %collective-permute-start.3 = (f32[8,256]{1,0:T(8,128)S(1)}, f32[8,256]{1,0:T(8,128)S(1)}, u32[]{:S(2)}, u32[]{:S(2)}) collective-permute-start(f32[8,256]{1,0:T(8,128)S(1)} %reshape.142), channel_id=1, source_target_pairs={{8,0},{16,8},{24,16},{0,24},{9,1},{17,9},{25,17},{1,25},{10,2},{18... | collective-permute-start | bytes 24584 | tf_op jit(solution)/shard_map/ppermute | solution.py:42
  47.5 1.7 %copy-start.3 = (f32[2304,256]{1,0:T(8,128)S(1)}, f32[2304,256]{1,0:T(8,128)}, u32[]{:S(2)}) copy-start(f32[2304,256]{1,0:T(8,128)} %param.6) | copy-start | bytes 7077892
  49.2 2.9 %copy-start.6 = (f32[9,256,256]{2,1,0:T(8,128)S(1)}, f32[9,256,256]{2,1,0:T(8,128)}, u32[]{:S(2)}) copy-start(f32[9,256,256]{2,1,0:T(8,128)} %copy.30) | copy-start | bytes 7077892
  59.9 1.0 copy-start.8
  60.9 3.1 %slice-start = ((s8[4718592]{0:T(1024)(128)(4,1)}), s8[4194304]{0:T(1024)(128)(4,1)S(1)}, s32[]{:S(2)}) async-start(s8[4718592]{0:T(1024)(128)(4,1)} %bitcast.191), calls=%async_computation | async-start | bytes 8388608
  61.1 3.0 %slice-start.1 = ((s8[4718592]{0:T(1024)(128)(4,1)}), s8[524288]{0:T(1024)(128)(4,1)S(1)}, s32[]{:S(2)}) async-start(s8[4718592]{0:T(1024)(128)(4,1)} %bitcast.191), calls=%async_computation.1 | async-start | bytes 1048576
  63.8 16.1 %collective-permute-start.17 = (f32[2,2,32,2304]{3,2,1,0:T(8,128)S(1)}, f32[2,2,32,2304]{3,2,1,0:T(8,128)S(1)}, u32[]{:S(2)}, u32[]{:S(2)}) collective-permute-start(f32[2,2,32,2304]{3,2,1,0:T(8,128)S(1)} %bitcast.213), channel_id=1, source_target_pairs={{0,2},{1,3},{2,0},{3,1},{4,6},{5,7},{6,4},{7,5},{8,10},{9,11},{10,... | collective-permute-start | bytes 3538952 | tf_op jit(solution)/shard_map/ppermute | solution.py:117
  67.4 3.4 %copy-start.4 = (f32[2304,256]{1,0:T(8,128)S(1)}, f32[2304,256]{1,0:T(8,128)}, u32[]{:S(2)}) copy-start(f32[2304,256]{1,0:T(8,128)} %param.7) | copy-start | bytes 7077892
  67.4 3.4 %copy-start.7 = (f32[1,16,32,256]{3,2,1,0:T(8,128)S(1)}, f32[1,16,32,256]{3,2,1,0:T(8,128)}, u32[]{:S(2)}) copy-start(f32[1,16,32,256]{3,2,1,0:T(8,128)} %param.4) | copy-start | bytes 1572868
  67.6 14.2 %collective-permute-start.12 = (f32[2,2,32,2304]{3,2,1,0:T(8,128)S(1)}, f32[2,2,32,2304]{3,2,1,0:T(8,128)S(1)}, u32[]{:S(2)}, u32[]{:S(2)}) collective-permute-start(f32[2,2,32,2304]{3,2,1,0:T(8,128)S(1)} %bitcast.214), channel_id=1, source_target_pairs={{0,2},{1,3},{2,0},{3,1},{4,6},{5,7},{6,4},{7,5},{8,10},{9,11},{10,... | collective-permute-start | bytes 3538952 | tf_op jit(solution)/shard_map/ppermute | solution.py:117
  70.8 3.8 %copy-start.1 = (f32[1,16,32,256]{3,2,1,0:T(8,128)S(1)}, f32[1,16,32,256]{3,2,1,0:T(8,128)}, u32[]{:S(2)}) copy-start(f32[1,16,32,256]{3,2,1,0:T(8,128)} %param.5) | copy-start | bytes 1572868
  70.8 3.8 %copy-start.5 = (f32[9,256,256]{2,1,0:T(8,128)S(1)}, f32[9,256,256]{2,1,0:T(8,128)}, u32[]{:S(2)}) copy-start(f32[9,256,256]{2,1,0:T(8,128)} %copy.31) | copy-start | bytes 7077892
  80.2 16.0 %collective-permute-start.18 = (f32[2,32,2304]{2,1,0:T(8,128)S(1)}, f32[2,32,2304]{2,1,0:T(8,128)S(1)}, u32[]{:S(2)}, u32[]{:S(2)}) collective-permute-start(f32[2,32,2304]{2,1,0:T(8,128)S(1)} %slice_bitcast_fusion), channel_id=1, source_target_pairs={{0,1},{1,0},{2,6},{3,7},{4,5},{5,4},{6,2},{7,3},{8,9},{9,8},{10,14... | collective-permute-start | bytes 1769480 | tf_op jit(solution)/shard_map/ppermute | solution.py:118
  81.9 15.7 %collective-permute-start.13 = (f32[2,32,2304]{2,1,0:T(8,128)S(1)}, f32[2,32,2304]{2,1,0:T(8,128)S(1)}, u32[]{:S(2)}, u32[]{:S(2)}) collective-permute-start(f32[2,32,2304]{2,1,0:T(8,128)S(1)} %slice_bitcast_fusion.2), channel_id=1, source_target_pairs={{0,4},{1,5},{2,3},{3,2},{4,0},{5,1},{6,7},{7,6},{8,12},{9,13},{10,... | collective-permute-start | bytes 1769480 | tf_op jit(solution)/shard_map/ppermute | solution.py:118
  96.2 9.1 %collective-permute-start.19 = (f32[32,2304]{1,0:T(8,128)S(1)}, f32[32,2304]{1,0:T(8,128)S(1)}, u32[]{:S(2)}, u32[]{:S(2)}) collective-permute-start(f32[32,2304]{1,0:T(8,128)S(1)} %slice_bitcast_fusion.4), channel_id=1, source_target_pairs={{0,4},{1,5},{2,3},{3,2},{4,0},{5,1},{6,7},{7,6},{8,12},{9,13},{10,... | collective-permute-start | bytes 884744 | tf_op jit(solution)/shard_map/ppermute | solution.py:119
  97.8 8.3 %collective-permute-start.14 = (f32[32,2304]{1,0:T(8,128)S(1)}, f32[32,2304]{1,0:T(8,128)S(1)}, u32[]{:S(2)}, u32[]{:S(2)}) collective-permute-start(f32[32,2304]{1,0:T(8,128)S(1)} %slice_bitcast_fusion.6), channel_id=1, source_target_pairs={{0,1},{1,0},{2,6},{3,7},{4,5},{5,4},{6,2},{7,3},{8,9},{9,8},{10,14... | collective-permute-start | bytes 884744 | tf_op jit(solution)/shard_map/ppermute | solution.py:119
  106.0 7.9 %collective-permute-start.20 = (f32[2,32,576]{2,1,0:T(8,128)S(1)}, f32[2,32,576]{2,1,0:T(8,128)S(1)}, u32[]{:S(2)}, u32[]{:S(2)}) collective-permute-start(f32[2,32,576]{2,1,0:T(8,128)S(1)} %pad_maximum_fusion.1), channel_id=1, source_target_pairs={{0,8},{2,18},{4,12},{6,22},{8,0},{10,26},{12,4},{14,30},{16,24},{1... | collective-permute-start | bytes 442376 | tf_op jit(solution)/shard_map/ppermute | solution.py:137
  106.8 9.2 %collective-permute-start.15 = (f32[2,32,576]{2,1,0:T(8,128)S(1)}, f32[2,32,576]{2,1,0:T(8,128)S(1)}, u32[]{:S(2)}, u32[]{:S(2)}) collective-permute-start(f32[2,32,576]{2,1,0:T(8,128)S(1)} %pad_maximum_fusion), channel_id=1, source_target_pairs={{0,16},{2,10},{4,20},{6,14},{8,24},{10,2},{12,28},{14,6},{16,0},{1... | collective-permute-start | bytes 442376 | tf_op jit(solution)/shard_map/ppermute | solution.py:137
  113.9 5.4 %collective-permute-start.21 = (f32[32,576]{1,0:T(8,128)S(1)}, f32[32,576]{1,0:T(8,128)S(1)}, u32[]{:S(2)}, u32[]{:S(2)}) collective-permute-start(f32[32,576]{1,0:T(8,128)S(1)} %slice_bitcast_fusion.8), channel_id=1, source_target_pairs={{0,16},{2,10},{4,20},{6,14},{8,24},{10,2},{12,28},{14,6},{16,0},{1... | collective-permute-start | bytes 221192 | tf_op jit(solution)/shard_map/ppermute | solution.py:138
  116.0 4.5 %collective-permute-start.16 = (f32[32,576]{1,0:T(8,128)S(1)}, f32[32,576]{1,0:T(8,128)S(1)}, u32[]{:S(2)}, u32[]{:S(2)}) collective-permute-start(f32[32,576]{1,0:T(8,128)S(1)} %slice_bitcast_fusion.10), channel_id=1, source_target_pairs={{0,8},{2,18},{4,12},{6,22},{8,0},{10,26},{12,4},{14,30},{16,24},{1... | collective-permute-start | bytes 221192 | tf_op jit(solution)/shard_map/ppermute | solution.py:138
